TPU v7x, 32 devices: a whole 2x2x4 slice. The times are simulated.
32 devices in a mesh: dp: 8 (over z, y), table: 2 (over x), rep: 2 (over core).
Axes of the slice: x: 2, y: 2, z: 4, core: 2. Of those that a mesh axis runs over, the one named last changes fastest.
Arguments:
- item_table: bfloat16 [3072, 256], P('table'), may hold values from -6 to 6
- fetch_rows: int32 [32, 192], P(('dp', 'table', 'rep')), may hold values from 0 to 1535, as said below
- fetch_count: int32 [32, 2], P(('dp', 'table', 'rep')), may hold values from 1 to 96, as said below
- item_slot: int32 [12288], P(('dp', 'table', 'rep')), may hold values from 0 to 191, as said below
- action_id: int32 [12288], P(('dp', 'table', 'rep')), may hold values from 0 to 15
- lengths: int32 [32, 8], P(('dp', 'table', 'rep')), may hold values from 1 to 192, as said below
- action_table: bfloat16 [16, 256], replicated, may hold values from -6 to 6
- w_in: bfloat16 [256, 1024], replicated, may hold values from -0.375 to 0.375
- w_proj: bfloat16 [1024, 1024], replicated, may hold values from -0.1875 to 0.1875
- w_out: bfloat16 [256, 1024], replicated, may hold values from -0.375 to 0.375
- cotangent: bfloat16 [12288, 1024], P(('dp', 'table', 'rep')), may hold values from -6 to 6
Outputs:
- item_grad: float32 [49152, 256], P(('dp', 'table', 'rep'))
- grad_w_in: float32 [256, 1024], P('table')
- grad_proj: float32 [1024, 1024], P('table')
- grad_out: float32 [256, 1024], P('table')
- grad_action: float32 [16, 256], P(None, 'table')
Inputs may be any that keep to these rules, and one draw needn't show every extreme that they name: `fetch_rows`: the 96 rows that one device may send to one requester are distinct. `fetch_count`: in every group of devices that share the dp and rep index, some requester receives 96 rows from every owner. `item_slot`: an event's slot lies within the rows its owner sends: owner times 96 plus a slot below that owner's count for this device. Each device's 8 lengths sum to at most 384; some device's sum to exactly 384.
All inputs are finite; a program needn't handle non-finite values.
Results may differ from a plain program's by a relative error of at most 0.012.
Values may be sent and summed in bfloat16 or wider, within the bound.
A program may use at most 64 MiB of HBM per device.

v0:
```python
import jax
import jax.numpy as jnp
from jax import lax
from jax.sharding import PartitionSpec as P

HEADS = 2
HEAD = 128


epsilon = 1e-05


def layer_norm(matrix):
    center = matrix - jnp.mean(matrix, axis=-1, keepdims=True)
    spread = jnp.mean(center * center, axis=-1, keepdims=True)
    return center * lax.rsqrt(spread + epsilon)


def sequence_layout(lengths, count):
    ends = jnp.cumsum(lengths, dtype=jnp.int32)
    position = jnp.arange(count, dtype=jnp.int32)
    live = position < ends[-1]
    sequence = jnp.sum(
        (position[:, None] >= ends[None, :]).astype(jnp.int32), axis=1, dtype=jnp.int32
    )
    chosen = sequence[:, None] == jnp.arange(lengths.shape[0], dtype=jnp.int32)[None, :]
    row_length = jnp.sum(jnp.where(chosen, lengths[None, :], 0), axis=1, dtype=jnp.int32)
    allowed = (sequence[:, None] == sequence[None, :]) & (position[None, :] <= position[:, None])
    allowed = allowed & live[:, None] & live[None, :]
    safe_length = jnp.maximum(row_length, 1).astype(jnp.float32)
    inverse_length = jnp.where(live, 1.0 / safe_length, jnp.zeros_like(safe_length))
    return (allowed, inverse_length, live)


def mixing(projected, allowed, inverse_length, heads, head):
    width = heads * head
    count = projected.shape[0]
    activated = jax.nn.silu(projected)
    gating = activated[:, :width].astype(jnp.bfloat16)
    value_rows = activated[:, width : 2 * width].astype(jnp.bfloat16)
    queries = activated[:, 2 * width : 3 * width].astype(jnp.bfloat16)
    key_rows = activated[:, 3 * width :].astype(jnp.bfloat16)
    query_heads = queries.reshape(count, heads, head)
    key_heads = key_rows.reshape(count, heads, head)
    value_heads = value_rows.reshape(count, heads, head)
    scores = jnp.einsum(
        "thd,shd->hts", query_heads, key_heads, preferred_element_type=jnp.float32
    ) * head ** (-0.5)
    weights = jnp.where(allowed[None], jax.nn.silu(scores), 0.0) * inverse_length[None, :, None]
    weights = weights.astype(jnp.bfloat16)
    attended = jnp.einsum(
        "hts,shd->thd", weights, value_heads, preferred_element_type=jnp.float32
    ).reshape(count, width)
    return (layer_norm(attended) * gating.astype(jnp.float32)).astype(jnp.bfloat16)


def local_terms(
    fetched, item_slot, action_id, lengths, action_table, w_in, w_proj, w_out, cotangent
):
    count = cotangent.shape[0]
    loss_scale = count ** (-0.5)
    allowed, inverse_length, live = sequence_layout(lengths, count)
    cotangent = jnp.where(live[:, None], cotangent, jnp.zeros_like(cotangent))
    item_rows = jnp.take(fetched, item_slot, axis=0)
    action_hot = action_id[:, None] == jnp.arange(action_table.shape[0], dtype=jnp.int32)[None, :]
    action_rows = jnp.dot(
        action_hot.astype(jnp.bfloat16), action_table, preferred_element_type=jnp.float32
    )
    embedded = (item_rows.astype(jnp.float32) + action_rows).astype(jnp.bfloat16)
    hidden = jnp.dot(embedded, w_in, preferred_element_type=jnp.float32)
    normed_full, norm_back = jax.vjp(layer_norm, hidden)
    normed = normed_full.astype(jnp.bfloat16)
    projected = jnp.dot(normed, w_proj, preferred_element_type=jnp.float32)
    mixed_rows, mix_back = jax.vjp(
        lambda values: mixing(values, allowed, inverse_length, HEADS, HEAD), projected
    )
    grad_out = jnp.dot(mixed_rows.T, cotangent, preferred_element_type=jnp.float32) * loss_scale
    grad_mixed = (
        jnp.dot(cotangent, w_out.T, preferred_element_type=jnp.float32) * loss_scale
    ).astype(jnp.bfloat16)
    grad_pre = mix_back(grad_mixed)[0].astype(jnp.bfloat16)
    grad_proj = jnp.dot(normed.T, grad_pre, preferred_element_type=jnp.float32)
    grad_normed = jnp.dot(grad_pre, w_proj.T, preferred_element_type=jnp.float32)
    grad_hidden = (cotangent.astype(jnp.float32) * loss_scale + norm_back(grad_normed)[0]).astype(
        jnp.bfloat16
    )
    grad_in = jnp.dot(embedded.T, grad_hidden, preferred_element_type=jnp.float32)
    grad_embedded = jnp.dot(grad_hidden, w_in.T, preferred_element_type=jnp.float32)
    slot_hot = (
        item_slot[:, None] == jnp.arange(fetched.shape[0], dtype=jnp.int32)[None, :]
    ).astype(jnp.float32)
    slot_grad = jnp.dot(slot_hot.T, grad_embedded, precision=lax.Precision.HIGHEST)
    action_grad = jnp.dot(
        action_hot.astype(jnp.float32).T, grad_embedded, precision=lax.Precision.HIGHEST
    )
    return ((grad_in, grad_proj, grad_out, action_grad), slot_grad)


def shards(
    item_table,
    fetch_rows,
    fetch_count,
    item_slot,
    action_id,
    lengths,
    action_table,
    w_in,
    w_proj,
    w_out,
    cotangent,
):
    table_count = lax.axis_size("table")
    fetched_count = fetch_rows.shape[1]
    slot_count = fetched_count // table_count
    width = item_table.shape[1]
    valid = jnp.arange(slot_count, dtype=jnp.int32)[None, :] < fetch_count[0][:, None]
    taken = jnp.take(item_table, fetch_rows[0], axis=0).reshape(table_count, slot_count, width)
    outgoing = jnp.where(valid[:, :, None], taken, jnp.zeros_like(taken))
    fetched = lax.all_to_all(outgoing, "table", split_axis=0, concat_axis=0, tiled=True).reshape(
        fetched_count, width
    )
    dense, slot_grad = local_terms(
        fetched, item_slot, action_id, lengths[0], action_table, w_in, w_proj, w_out, cotangent
    )
    returned = lax.all_to_all(
        slot_grad.reshape(table_count, slot_count, width),
        "table",
        split_axis=0,
        concat_axis=0,
        tiled=True,
    )
    returned = jnp.where(valid[:, :, None], returned, jnp.zeros_like(returned))
    item_grad = (
        jnp.zeros((item_table.shape[0], width), jnp.float32)
        .at[fetch_rows[0]]
        .add(returned.reshape(fetched_count, width))
    )
    factor = (lax.axis_size("dp") * table_count * lax.axis_size("rep")) ** (-0.5)
    grad_in = dense[0] * factor
    grad_proj = dense[1] * factor
    grad_out = dense[2] * factor
    action_grad = dense[3] * factor
    shares = (
        lax.psum_scatter(grad_in, "table", scatter_dimension=0, tiled=True),
        lax.psum_scatter(grad_proj, "table", scatter_dimension=0, tiled=True),
        lax.psum_scatter(grad_out, "table", scatter_dimension=0, tiled=True),
        lax.psum_scatter(action_grad, "table", scatter_dimension=1, tiled=True),
    )
    totals = lax.psum((shares[0], shares[1], shares[2], shares[3]), ("dp", "rep"))
    return (item_grad, totals[0], totals[1], totals[2], totals[3])


def solution(mesh):
    return jax.shard_map(
        shards,
        mesh=mesh,
        in_specs=(
            P("table", None),
            P(("dp", "table", "rep"), None),
            P(("dp", "table", "rep"), None),
            P(("dp", "table", "rep")),
            P(("dp", "table", "rep")),
            P(("dp", "table", "rep"), None),
            P(),
            P(),
            P(),
            P(),
            P(("dp", "table", "rep"), None),
        ),
        out_specs=(
            P(("dp", "table", "rep"), None),
            P("table", None),
            P("table", None),
            P("table", None),
            P(None, "table"),
        ),
        check_vma=False,
    )
```

profile of v0, /device:TPU:1, one launch (start us, length us, event | category | flops | bytes accessed | tf_op | source)
XLA Modules:
  0.0 268.9 jit_solution(15628239672412625532)
XLA Ops:
  7.2 0.8 compare_select_fusion
  8.0 0.5 broadcast.256
  8.5 1.3 reduce.6
  10.0 0.7 compare_and_fusion
  10.7 2.1 gather_fusion
  12.8 0.8 select_select_fusion
  13.6 3.3 %all-to-all-start = ((bf16[2,96,256]{2,1,0:T(8,128)(2,1)}), bf16[2,96,256]{2,1,0:T(8,128)(2,1)S(1)}, u32[]{:S(2)}, u32[]{:S(2)}) async-start(bf16[2,96,256]{2,1,0:T(8,128)(2,1)} %select_select_fusion), calls=%async_computation | async-start | bytes 196608 | tf_op jit(solution)/shard_map/all_to_all | solution.py:119
  17.0 0.7 compare_and_fusion.1
  17.7 0.7 compare_select_fusion.1
  18.4 0.8 reduce-window.4
  19.2 0.6 slice.20
  19.8 0.6 iota_compare_fusion.8
  20.5 0.7 select_reduce_fusion
  21.3 0.6 divide_select_fusion
  22.1 2.1 gather_fusion.1
  24.5 0.5 fusion.30
  25.0 0.3 multiply_reduce_fusion.1
  25.3 2.7 multiply_convert_fusion
  28.0 0.7 multiply_convert_fusion.2
  28.8 0.3 fusion.31
  29.2 0.7 copy-done.3
  30.0 0.6 multiply_reduce_fusion.2
  31.0 0.3 fusion.37
  31.5 0.7 fusion.8
  32.3 1.0 fusion.35
  33.3 1.5 convolution_multiply_fusion.2
  34.9 0.3 fusion.36
  35.2 3.5 %multiply_reduce_fusion = (f32[384]{0:T(512)S(1)}, f32[384,1024]{1,0:T(8,128)S(1)}) fusion(f32[384,1024]{1,0:T(8,128)} %copy-done.1, f32[384]{0:T(512)S(1)} %broadcast_multiply_fusion.1, bf16[1024,1024]{1,0:T(8,128)(2,1)S(1)} %copy-done, f32[384,1024]{0,1:T(8,128)} %get-tuple-element.21, bf16[384,256]{0,1:T(8,128)(2,1)S(1)} %get-tuple-element.12, ...), kind=kOutput, calls=%fused_computation.11 | convolution fusion | flops 813170304 | bytes 7605248 | tf_op jit(solution)/shard_map/dot_general | solution.py:83
  38.8 0.5 fusion.28
  39.3 0.6 copy-done.4
  39.9 0.4 add_convert_fusion
  40.3 1.4 convolution_multiply_fusion.3
  42.0 5.5 %convolution_multiply_fusion = f32[1024,1024]{1,0:T(8,128)} fusion(f32[384,1024]{1,0:T(8,128)} %copy-done.1, f32[384]{0:T(512)S(1)} %fusion.24, f32[384]{0:T(512)S(1)} %broadcast_multiply_fusion.1, f32[384,1024]{0,1:T(8,128)} %get-tuple-element.21, bf16[384,256]{0,1:T(8,128)(2,1)S(1)} %copy-done.8, bf16[384,256]{0,1:T(8,128)(2,1)S(1)} %bitcast.85, ...), kind=kOutput, calls=%fused_computation.5 | convolution fusion | flops 814219264 | bytes 8129536 | tf_op jit(solution)/shard_map/dot_general | solution.py:82
  47.6 1.4 fusion.34
  49.0 1.0 convolution_multiply_fusion.5
  50.1 7.7 %reduce-scatter.9.cloned.1.call-done = f32[128,1024]{1,0:T(8,128)} async-done(((f32[256,1024]{1,0:T(8,128)}), f32[128,1024]{1,0:T(8,128)}) %reduce-scatter.9.cloned.1.call-update) | async-done | bytes 524304 | tf_op jit(solution)/shard_map/reduce_scatter | solution.py:146
  57.8 22.7 %reduce-scatter.5.cloned.1.call-done = f32[128,1024]{1,0:T(8,128)} async-done(((f32[256,1024]{1,0:T(8,128)}), f32[128,1024]{1,0:T(8,128)}) %reduce-scatter.5.cloned.1.call-update) | async-done | bytes 524304 | tf_op jit(solution)/shard_map/reduce_scatter | solution.py:144
  80.5 56.6 %reduce-scatter.7.cloned.1.call-done = f32[512,1024]{1,0:T(8,128)} async-done(((f32[1024,1024]{1,0:T(8,128)}), f32[512,1024]{1,0:T(8,128)}) %reduce-scatter.7.cloned.1.call-update) | async-done | bytes 2097168 | tf_op jit(solution)/shard_map/reduce_scatter | solution.py:145
  137.2 0.7 copy-done.14
  137.8 1.3 fusion.20
  139.1 3.4 %all-to-all-start.1 = ((f32[2,96,256]{2,1,0:T(8,128)}), f32[2,96,256]{2,1,0:T(8,128)S(1)}, u32[]{:S(2)}, u32[]{:S(2)}) async-start(f32[2,96,256]{2,1,0:T(8,128)} %bitcast.23), calls=%async_computation.1 | async-start | bytes 393216 | tf_op jit(solution)/shard_map/all_to_all | solution.py:125
  142.6 6.6 %reduce-scatter.11.cloned.1.call-done = f32[16,128]{1,0:T(8,128)} async-done(((f32[16,256]{1,0:T(8,128)}), f32[16,128]{1,0:T(8,128)}) %reduce-scatter.11.cloned.1.call-update) | async-done | bytes 8208 | tf_op jit(solution)/shard_map/reduce_scatter | solution.py:147
  149.2 31.9 %psum.31 = f32[16,128]{1,0:T(8,128)} all-reduce(f32[16,128]{1,0:T(8,128)} %reduce-scatter.11.cloned.1.call-done), channel_id=1, replica_groups=mesh['dp'=8,'table'=2,'rep'=2] {'dp','rep'}, use_global_device_ids=true, to_apply=%region_19.20 | all-reduce | flops 2048 | bytes 16384 | tf_op jit(solution)/shard_map/psum | solution.py:149
  181.2 2.8 %scatter_custom_fusion = f32[1536,256]{1,0:T(8,128)} fusion(s32[192]{0:T(256)S(1)} %bitcast.91, f32[192,256]{1,0:T(8,128)S(1)} %bitcast.83, f32[]{:T(128)} %constant.27.clone.1), kind=kCustom, calls=%fused_computation.37 | custom fusion | flops 49152 | bytes 1572868 | tf_op jit(solution)/shard_map/scatter-add | solution.py:136
  184.0 72.5 %all-reduce.7.cloned.1.call-done = (f32[128,1024]{1,0:T(8,128)}, f32[512,1024]{1,0:T(8,128)}, f32[128,1024]{1,0:T(8,128)}) async-done(((f32[128,1024]{1,0:T(8,128)}, f32[512,1024]{1,0:T(8,128)}, f32[128,1024]{1,0:T(8,128)}), (f32[128,1024]{1,0:T(8,128)}, f32[512,1024]{1,0:T(8,128)}, f32[128,1024]{1,0:T(8,128)})) %all-reduce.7.cloned.1.call-update) | async-done | bytes 3145744 | tf_op jit(solution)/shard_map/psum | solution.py:149
  256.4 1.9 copy.45
  258.3 3.2 %copy.46 = f32[512,1024]{1,0:T(8,128)} copy(f32[512,1024]{1,0:T(8,128)} %get-tuple-element.34) | data formatting | bytes 4194304
  261.5 0.8 copy.47
  (63 shorter events, 2.2 us)
Async XLA Ops:
  7.2 18.1 %copy-start = (bf16[1024,1024]{1,0:T(8,128)(2,1)S(1)}, bf16[1024,1024]{1,0:T(8,128)(2,1)}, u32[]{:S(2)}) copy-start(bf16[1024,1024]{1,0:T(8,128)(2,1)} %param.19) | copy-start | bytes 6291460
  10.7 13.5 %copy-start.15 = (s32[384]{0:T(512)S(1)}, s32[384]{0:T(512)}, u32[]{:S(2)}) copy-start(s32[384]{0:T(512)} %param.15) | copy-start | bytes 4612
  10.7 13.5 %copy-start.17 = (bf16[16,256]{1,0:T(8,128)(2,1)S(1)}, bf16[16,256]{1,0:T(8,128)(2,1)}, u32[]{:S(2)}) copy-start(bf16[16,256]{1,0:T(8,128)(2,1)} %param.17) | copy-start | bytes 24580
  12.8 11.7 %copy-start.5 = (bf16[256,1024]{1,0:T(8,128)(2,1)S(1)}, bf16[256,1024]{1,0:T(8,128)(2,1)}, u32[]{:S(2)}) copy-start(bf16[256,1024]{1,0:T(8,128)(2,1)} %param.18) | copy-start | bytes 1572868
  13.6 8.5 %all-to-all-start = ((bf16[2,96,256]{2,1,0:T(8,128)(2,1)}), bf16[2,96,256]{2,1,0:T(8,128)(2,1)S(1)}, u32[]{:S(2)}, u32[]{:S(2)}) async-start(bf16[2,96,256]{2,1,0:T(8,128)(2,1)} %select_select_fusion), calls=%async_computation | async-start | bytes 196608 | tf_op jit(solution)/shard_map/all_to_all | solution.py:119
  16.9 40.9 %reduce-scatter.9.cloned.1.call-start = ((), (), s32[]{:S(2)}) async-start(), calls=%async_computation.8 | async-start | bytes 1572864 | tf_op jit(solution)/shard_map/reduce_scatter | solution.py:146
  22.1 5.9 %copy-start.12 = (pred[384,384]{1,0:T(8,128)(4,1)}, pred[384,384]{1,0:T(8,128)(4,1)S(1)}, u32[]{:S(2)}) copy-start(pred[384,384]{1,0:T(8,128)(4,1)S(1)} %fusion.16) | copy-start | bytes 442372
  25.0 3.0 %copy-start.1 = (f32[384,1024]{1,0:T(8,128)}, f32[384,1024]{1,0:T(8,128)S(1)}, u32[]{:S(2)}) copy-start(f32[384,1024]{1,0:T(8,128)S(1)} %get-tuple-element.19) | copy-start | bytes 4718596
  28.8 1.1 copy-start.3
  28.8 1.3 copy-start.16
  30.6 0.9 copy-start.13
  30.8 4.4 %copy-start.7 = (bf16[384,256]{0,1:T(8,128)(2,1)}, bf16[384,256]{0,1:T(8,128)(2,1)S(1)}, u32[]{:S(2)}) copy-start(bf16[384,256]{0,1:T(8,128)(2,1)S(1)} %get-tuple-element.12) | copy-start | bytes 589828
  31.2 3.9 %copy-start.9 = (bf16[2,128,384]{2,1,0:T(8,128)(2,1)}, bf16[2,128,384]{2,1,0:T(8,128)(2,1)S(1)}, u32[]{:S(2)}) copy-start(bf16[2,128,384]{2,1,0:T(8,128)(2,1)S(1)} %fusion.37) | copy-start | bytes 589828
  34.8 45.7 %reduce-scatter.5.cloned.1.call-start = ((), (), s32[]{:S(2)}) async-start(), calls=%async_computation.6 | async-start | bytes 1572864 | tf_op jit(solution)/shard_map/reduce_scatter | solution.py:144
  35.2 3.6 %copy-start.11 = (bf16[2,384,128]{1,2,0:T(8,128)(2,1)}, bf16[2,384,128]{1,2,0:T(8,128)(2,1)S(1)}, u32[]{:S(2)}) copy-start(bf16[2,384,128]{1,2,0:T(8,128)(2,1)S(1)} %fusion.36) | copy-start | bytes 589828
  35.2 3.6 %copy-start.2 = (f32[384,1024]{1,0:T(8,128)S(1)}, f32[384,1024]{1,0:T(8,128)}, u32[]{:S(2)}) copy-start(f32[384,1024]{1,0:T(8,128)} %copy-done.1) | copy-start | bytes 4718596
  38.8 1.1 copy-start.4
  40.3 1.7 copy-start.8
  40.3 1.7 copy-start.10
  41.8 95.4 %reduce-scatter.7.cloned.1.call-start = ((), (), s32[]{:S(2)}) async-start(), calls=%async_computation.7 | async-start | bytes 6291456 | tf_op jit(solution)/shard_map/reduce_scatter | solution.py:145
  47.5 101.7 %reduce-scatter.11.cloned.1.call-start = ((), (), s32[]{:S(2)}) async-start(), calls=%async_computation.9 | async-start | bytes 24576 | tf_op jit(solution)/shard_map/reduce_scatter | solution.py:147
  50.0 206.4 %all-reduce.7.cloned.1.call-start = ((), (), s32[]{:S(2)}) async-start(), calls=%async_computation.10 | async-start | bytes 6291456 | tf_op jit(solution)/shard_map/psum | solution.py:149
  137.2 0.7 copy-start.14
  139.1 41.9 %all-to-all-start.1 = ((f32[2,96,256]{2,1,0:T(8,128)}), f32[2,96,256]{2,1,0:T(8,128)S(1)}, u32[]{:S(2)}, u32[]{:S(2)}) async-start(f32[2,96,256]{2,1,0:T(8,128)} %bitcast.23), calls=%async_computation.1 | async-start | bytes 393216 | tf_op jit(solution)/shard_map/all_to_all | solution.py:125
  258.3 3.2 %copy-start.6 = (f32[128,1024]{1,0:T(8,128)S(1)}, f32[128,1024]{1,0:T(8,128)}, u32[]{:S(2)}) copy-start(f32[128,1024]{1,0:T(8,128)} %get-tuple-element.35) | copy-start | bytes 1572868
Sparse Core Ops, SparseCore 0:
  35.0 22.8 reduce-scatter.8
  60.2 20.3 reduce-scatter.4
  82.8 54.2 reduce-scatter.6
  139.8 9.2 reduce-scatter.10
  153.4 103.0 all-reduce.6
where the time goes:
time: 272 us; the launch traced here: 269 us
  waiting for transfers between devices  166 us (61%)
  blocking collectives  31.9 us (12%)
  matrix products  23 us (8%)
  between operations  14.2 us (5%)
  local copies, waits for them, and re-layouts  13.8 us (5%)
  other arithmetic  12.7 us (5%)
  starting transfers between devices  7.16 us (3%)
    psum x1, waiting for transfers between devices, shards(): lax.psum((shares[0], shares[1], shares[2], shares[3]), ('dp', 'rep'))  72.5 us
    reduce_scatter x1, waiting for transfers between devices, shards(): lax.psum_scatter(grad_proj, 'table', scatter_dimension=0, tiled=True)  56.6 us
    psum x1, blocking collectives, shards(): lax.psum((shares[0], shares[1], shares[2], shares[3]), ('dp', 'rep'))  31.9 us
    reduce_scatter x1, waiting for transfers between devices, shards(): lax.psum_scatter(grad_in, 'table', scatter_dimension=0, tiled=True)  22.7 us
    unnamed x40, local copies, waits for them, and re-layouts  8.86 us
    reduce_scatter x1, waiting for transfers between devices, shards(): lax.psum_scatter(grad_out, 'table', scatter_dimension=0, tiled=True)  7.74 us
    reduce_scatter x1, waiting for transfers between devices, shards(): lax.psum_scatter(action_grad, 'table', scatter_dimension=1, tiled=True)  6.6 us
    dot_general x1, matrix products, local_terms(): grad_proj = jnp.dot(normed.T, grad_pre, preferred_element_type=jnp.float32)  5.45 us
  transfers between devices with their start and end apart: 7, of which 5 were waited for; matrix products, arithmetic and copies ran while one was open for 9% of the time, Pallas kernels for 0%

commit v1 on v0

--- a/solution.py
+++ b/solution.py
@@ -1,6 +1,8 @@
 import jax
 import jax.numpy as jnp
 from jax import lax
+from jax.experimental import pallas as pl
+from jax.experimental.pallas import tpu as pltpu
 from jax.sharding import PartitionSpec as P
 
 HEADS = 2
@@ -94,6 +96,227 @@
         action_hot.astype(jnp.float32).T, grad_embedded, precision=lax.Precision.HIGHEST
     )
     return ((grad_in, grad_proj, grad_out, action_grad), slot_grad)
+
+
+CHUNKS = 4
+
+
+def flip(axis, bit):
+    at = lax.axis_index(axis)
+    return jnp.bitwise_xor(at, 1 << bit), jnp.bitwise_and(at // (1 << bit), 1)
+
+
+def combine_kernel(
+    dp_bits,
+    proj_ref,
+    in_ref,
+    out_ref,
+    action_ref,
+    slot_ref,
+    proj_o,
+    in_o,
+    out_o,
+    action_o,
+    slot_o,
+    work,
+    final,
+    action_acc,
+    action_got,
+    slot_got,
+    *rest,
+):
+    got = rest[: dp_bits + 2]
+    send_sem, recv_sem, gather_send, gather_recv, action_send, action_recv, slot_send, slot_recv = rest[
+        dp_bits + 2 :
+    ]
+    chunks, _, rows, columns = work.shape
+    table = lax.axis_index("table")
+    other_table = 1 - table
+    steps = [("rep", *flip("rep", 0)), ("table", *flip("table", 0))]
+    steps += [("dp", *flip("dp", bit)) for bit in range(dp_bits)]
+
+    barrier = pltpu.get_barrier_semaphore()
+    for axis, partner, _ in steps:
+        pl.semaphore_signal(
+            barrier, inc=1, device_id={axis: partner}, device_id_type=pl.DeviceIdType.MESH
+        )
+    pl.semaphore_wait(barrier, len(steps))
+
+    def remote(src, dst, send, recv, step):
+        axis, partner, _ = steps[step]
+        return pltpu.make_async_remote_copy(
+            src_ref=src,
+            dst_ref=dst,
+            send_sem=send,
+            recv_sem=recv,
+            device_id={axis: partner},
+            device_id_type=pl.DeviceIdType.MESH,
+        )
+
+    starts, counts = [0], [rows]
+    sent = []
+    halving = [0] + list(range(2, dp_bits + 2))
+    for step in halving:
+        half = counts[-1] // 2
+        own = steps[step][2]
+        sent.append(pl.multiple_of(starts[-1] + (1 - own) * half, 16))
+        starts.append(pl.multiple_of(starts[-1] + own * half, 16))
+        counts.append(half)
+
+    slot_copy = remote(slot_ref.at[other_table], slot_got, slot_send, slot_recv, 1)
+    slot_copy.start()
+    action_acc[0] = action_ref[...]
+
+    def action_copy(step):
+        if step == 0:
+            src, dst = action_acc.at[0], action_got.at[0]
+        elif step == 1:
+            src, dst = action_acc.at[1, other_table], action_got.at[1, 0]
+        else:
+            src, dst = action_acc.at[step, 0], action_got.at[step, 0]
+        return remote(src, dst, action_send.at[step], action_recv.at[step], step)
+
+    def action_add(step):
+        if step == 0:
+            action_acc[1] = action_acc[0] + action_got[0]
+        elif step == 1:
+            action_acc[2, 0] = action_acc[1, table] + action_got[1, 0]
+        else:
+            action_acc[step + 1, 0] = action_acc[step, 0] + action_got[step, 0]
+
+    def reduce_copy(chunk, step):
+        if step == 0:
+            src = work.at[chunk, :, pl.ds(sent[0], counts[1])]
+        elif step == 1:
+            src = work.at[chunk, other_table, pl.ds(starts[1], counts[1])]
+        else:
+            src = work.at[chunk, table, pl.ds(sent[step - 1], counts[step])]
+        return remote(
+            src, got[step].at[chunk], send_sem.at[chunk, step], recv_sem.at[chunk, step], step
+        )
+
+    def reduce_add(chunk, step):
+        part = max(step, 1)
+        if step == 0:
+            at = (chunk, slice(None), pl.ds(starts[1], counts[1]))
+        else:
+            at = (chunk, table, pl.ds(starts[part], counts[part]))
+        total = work[at].astype(jnp.float32) + got[step][chunk].astype(jnp.float32)
+        if step == dp_bits + 1:
+            final[chunk, pl.ds(starts[part], counts[part])] = total.astype(jnp.bfloat16)
+        else:
+            work[at] = total.astype(jnp.bfloat16)
+
+    backward = list(reversed(range(len(halving))))
+
+    def gather_copy(chunk, place):
+        at = backward[place]
+        piece = final.at[chunk, pl.ds(starts[at + 1], counts[at + 1])]
+        return remote(
+            piece, piece, gather_send.at[chunk, place], gather_recv.at[chunk, place], halving[at]
+        )
+
+    reduces, gathers = len(steps), len(backward)
+    half_proj, half_in, half_out = proj_ref.shape[0] // 2, in_ref.shape[0] // 2, out_ref.shape[0] // 2
+    for chunk in range(chunks):
+        wide = slice(chunk * columns, (chunk + 1) * columns)
+        for side in range(2):
+            work[chunk, side, :half_proj] = proj_ref[side * half_proj : (side + 1) * half_proj, wide]
+            work[chunk, side, half_proj : half_proj + half_in] = in_ref[
+                side * half_in : (side + 1) * half_in, wide
+            ]
+            work[chunk, side, half_proj + half_in :] = out_ref[
+                side * half_out : (side + 1) * half_out, wide
+            ]
+        reduce_copy(chunk, 0).start()
+    action_copy(0).start()
+
+    for wave in range(chunks + reduces + gathers - 1):
+        for chunk in range(chunks):
+            at = wave - chunk
+            if at < 0 or at >= reduces + gathers:
+                continue
+            if at < reduces:
+                reduce_copy(chunk, at).wait_recv()
+                reduce_add(chunk, at)
+                if at + 1 < reduces:
+                    reduce_copy(chunk, at + 1).start()
+                else:
+                    gather_copy(chunk, 0).start()
+            else:
+                place = at - reduces
+                gather_copy(chunk, place).wait_recv()
+                if place + 1 < gathers:
+                    gather_copy(chunk, place + 1).start()
+                else:
+                    wide = slice(chunk * columns, (chunk + 1) * columns)
+                    proj_o[:, wide] = final[chunk, :half_proj].astype(jnp.float32)
+                    in_o[:, wide] = final[chunk, half_proj : half_proj + half_in].astype(jnp.float32)
+                    out_o[:, wide] = final[chunk, half_proj + half_in :].astype(jnp.float32)
+        if wave < reduces:
+            action_copy(wave).wait_recv()
+            action_add(wave)
+            if wave + 1 < reduces:
+                action_copy(wave + 1).start()
+
+    action_o[...] = action_acc[reduces, 0]
+    slot_copy.wait_recv()
+    slot_o[table] = slot_ref[table]
+    slot_o[other_table] = slot_got[...]
+    slot_copy.wait_send()
+    for step in range(reduces):
+        action_copy(step).wait_send()
+        for chunk in range(chunks):
+            reduce_copy(chunk, step).wait_send()
+    for place in range(gathers):
+        for chunk in range(chunks):
+            gather_copy(chunk, place).wait_send()
+
+
+def combine(grad_proj, grad_in, grad_out, action_parts, slot_parts, dp_bits):
+    wide = grad_proj.shape[1]
+    rows = (grad_proj.shape[0] + grad_in.shape[0] + grad_out.shape[0]) // 2
+    columns = wide // CHUNKS
+    steps = dp_bits + 2
+    _, actions, action_wide = action_parts.shape
+    got = [pltpu.VMEM((CHUNKS, 2, rows // 2, columns), jnp.bfloat16)]
+    got += [pltpu.VMEM((CHUNKS, rows // 2, columns), jnp.bfloat16)]
+    got += [
+        pltpu.VMEM((CHUNKS, rows >> (bit + 2), columns), jnp.bfloat16) for bit in range(dp_bits)
+    ]
+    dma = pltpu.SemaphoreType.DMA
+    vmem = pl.BlockSpec(memory_space=pltpu.VMEM)
+    return pl.pallas_call(
+        lambda *refs: combine_kernel(dp_bits, *refs),
+        out_shape=(
+            jax.ShapeDtypeStruct((grad_proj.shape[0] // 2, wide), jnp.float32),
+            jax.ShapeDtypeStruct((grad_in.shape[0] // 2, wide), jnp.float32),
+            jax.ShapeDtypeStruct((grad_out.shape[0] // 2, wide), jnp.float32),
+            jax.ShapeDtypeStruct((actions, action_wide), jnp.float32),
+            jax.ShapeDtypeStruct(slot_parts.shape, jnp.float32),
+        ),
+        in_specs=[vmem] * 5,
+        out_specs=(vmem,) * 5,
+        scratch_shapes=[
+            pltpu.VMEM((CHUNKS, 2, rows, columns), jnp.bfloat16),
+            pltpu.VMEM((CHUNKS, rows, columns), jnp.bfloat16),
+            pltpu.VMEM((steps + 1, 2, actions, action_wide), jnp.float32),
+            pltpu.VMEM((steps, 2, actions, action_wide), jnp.float32),
+            pltpu.VMEM(slot_parts.shape[1:], jnp.float32),
+            *got,
+            dma((CHUNKS, steps)),
+            dma((CHUNKS, steps)),
+            dma((CHUNKS, steps - 1)),
+            dma((CHUNKS, steps - 1)),
+            dma((steps,)),
+            dma((steps,)),
+            dma,
+            dma,
+        ],
+        compiler_params=pltpu.CompilerParams(
+            collective_id=0, has_side_effects=True, vmem_limit_bytes=40 * 2**20
+        ),
+    )(grad_proj, grad_in, grad_out, action_parts, slot_parts)
 
 
 def shards(
@@ -122,31 +345,47 @@
     dense, slot_grad = local_terms(
         fetched, item_slot, action_id, lengths[0], action_table, w_in, w_proj, w_out, cotangent
     )
-    returned = lax.all_to_all(
-        slot_grad.reshape(table_count, slot_count, width),
-        "table",
-        split_axis=0,
-        concat_axis=0,
-        tiled=True,
-    )
+    factor = (lax.axis_size("dp") * table_count * lax.axis_size("rep")) ** (-0.5)
+    grad_in = dense[0] * factor
+    grad_proj = dense[1] * factor
+    grad_out = dense[2] * factor
+    action_grad = dense[3] * factor
+    dp_count = lax.axis_size("dp")
+    dp_bits = dp_count.bit_length() - 1
+    rows = (grad_in.shape[0] + grad_proj.shape[0] + grad_out.shape[0]) // 2
+    pairs = table_count == 2 and lax.axis_size("rep") == 2 and dp_count == 1 << dp_bits
+    if pairs and rows % (16 << (dp_bits + 1)) == 0:
+        actions = action_grad.shape[0]
+        proj_total, in_total, out_total, action_total, returned = combine(
+            grad_proj.astype(jnp.bfloat16),
+            grad_in.astype(jnp.bfloat16),
+            grad_out.astype(jnp.bfloat16),
+            action_grad.reshape(actions, 2, width // 2).swapaxes(0, 1),
+            slot_grad.reshape(table_count, slot_count, width),
+            dp_bits,
+        )
+        totals = (in_total, proj_total, out_total, action_total)
+    else:
+        returned = lax.all_to_all(
+            slot_grad.reshape(table_count, slot_count, width),
+            "table",
+            split_axis=0,
+            concat_axis=0,
+            tiled=True,
+        )
+        shares = (
+            lax.psum_scatter(grad_in, "table", scatter_dimension=0, tiled=True),
+            lax.psum_scatter(grad_proj, "table", scatter_dimension=0, tiled=True),
+            lax.psum_scatter(grad_out, "table", scatter_dimension=0, tiled=True),
+            lax.psum_scatter(action_grad, "table", scatter_dimension=1, tiled=True),
+        )
+        totals = lax.psum((shares[0], shares[1], shares[2], shares[3]), ("dp", "rep"))
     returned = jnp.where(valid[:, :, None], returned, jnp.zeros_like(returned))
     item_grad = (
         jnp.zeros((item_table.shape[0], width), jnp.float32)
         .at[fetch_rows[0]]
         .add(returned.reshape(fetched_count, width))
     )
-    factor = (lax.axis_size("dp") * table_count * lax.axis_size("rep")) ** (-0.5)
-    grad_in = dense[0] * factor
-    grad_proj = dense[1] * factor
-    grad_out = dense[2] * factor
-    action_grad = dense[3] * factor
-    shares = (
-        lax.psum_scatter(grad_in, "table", scatter_dimension=0, tiled=True),
-        lax.psum_scatter(grad_proj, "table", scatter_dimension=0, tiled=True),
-        lax.psum_scatter(grad_out, "table", scatter_dimension=0, tiled=True),
-        lax.psum_scatter(action_grad, "table", scatter_dimension=1, tiled=True),
-    )
-    totals = lax.psum((shares[0], shares[1], shares[2], shares[3]), ("dp", "rep"))
     return (item_grad, totals[0], totals[1], totals[2], totals[3])
 
 

time: 272 us -> 95.2 us (0.35)
  waiting for transfers between devices: 166 us -> 0.01 us
  Pallas kernels: 0 us -> 53.7 us
  blocking collectives: 31.9 us -> 0 us
  between operations: 14.2 us -> 0.96 us
  matrix products: 23 us -> 10.5 us
  starting transfers between devices: 7.16 us -> 3.34 us
    reduce_scatter x4 -> x0, waiting for transfers between devices: 93.7 us -> none  [the longest x1 56.6 us: shards(): lax.psum_scatter(grad_proj, 'table', scatter_dimension=0, tiled=True)]
    psum x1 -> x0, waiting for transfers between devices: 72.5 us -> none  [shards(): lax.psum((shares[0], shares[1], shares[2], shares[3]), ('dp', 'rep'))]
    pallas_call x0 -> x1, Pallas kernels: none -> 53.7 us  [combine(): pl.pallas_call(lambda *refs: combine_kernel(dp_bits, *refs), out_shape=(j...]
    psum x1 -> x0, blocking collectives: 31.9 us -> none  [shards(): lax.psum((shares[0], shares[1], shares[2], shares[3]), ('dp', 'rep'))]
    dot_general x1, matrix products: 5.45 us -> 1.49 us  [local_terms(): grad_proj = jnp.dot(normed.T, grad_pre, preferred_element_type=jnp.float32)]
    all_to_all x1 -> x0, starting transfers between devices: 3.43 us -> none  [shards(): lax.all_to_all(slot_grad.reshape(table_count, slot_count, width), 'table'...]
    unnamed x40 -> x21, local copies, waits for them, and re-layouts: 8.86 us -> 8.07 us
  transfers between devices with their start and end apart: 7 -> 1, of which waited for: 5 -> 0; matrix products, arithmetic and copies ran while one was open for 9% -> 5% of each run, Pallas kernels for 0% -> 0%
where the time goes in v1:
time: 95.2 us; the launch traced here: 94.8 us
  Pallas kernels  53.7 us (56%)
  other arithmetic  13.3 us (14%)
  local copies, waits for them, and re-layouts  13 us (14%)
  matrix products  10.5 us (11%)
  starting transfers between devices  3.34 us (4%)
  between operations  0.96 us (1%)
    pallas_call x1, Pallas kernels, combine(): pl.pallas_call(lambda *refs: combine_kernel(dp_bits, *refs), out_shape=(j...  53.7 us
    unnamed x21, local copies, waits for them, and re-layouts  8.07 us
    all_to_all x1, starting transfers between devices, shards(): lax.all_to_all(outgoing, 'table', split_axis=0, concat_axis=0, tiled=True)  3.34 us
    scatter-add x1, other arithmetic, shards(): item_grad = jnp.zeros((item_table.shape[0], width), jnp.float32).at[fetch...  2.8 us
    gather x1, local copies, waits for them, and re-layouts, shards(): jnp.take(item_table, fetch_rows[0], axis=0)  2.12 us
    gather x1, local copies, waits for them, and re-layouts, local_terms(): item_rows = jnp.take(fetched, item_slot, axis=0)  2.06 us
  transfers between devices with their start and end apart: 1, of which 0 were waited for; matrix products, arithmetic and copies ran while one was open for 5% of the time, Pallas kernels for 0%

profile of v1, /device:TPU:1, one launch (start us, length us, event | category | flops | bytes accessed | tf_op | source)
XLA Modules:
  0.0 94.8 jit_solution(8899305435086747939)
XLA Ops:
  0.6 0.8 compare_select_fusion
  1.5 0.5 broadcast.256
  2.0 1.3 %reduce.6 = s32[192]{0:T(256)S(1)} reduce(s32[1,192]{1,0:T(1,128)} %param.12, s32[]{:T(128)} %broadcast.256), dimensions={0}, to_apply=%param.12.reduce_sub_computation.3 | reduce | bytes 1540 | tf_op args[1]
  3.4 0.7 compare_and_fusion
  4.2 2.1 %gather_fusion = bf16[192,256]{1,0:T(8,128)(2,1)S(1)} fusion(bf16[1536,256]{1,0:T(8,128)(2,1)} %param.11, s32[1024]{0:T(1024)S(1)} %pad_clamp_fusion.1), kind=kCustom, calls=%fused_computation | custom fusion | bytes 197376 | tf_op jit(solution)/shard_map/jit(_take)/gather | solution.py:340
  6.3 0.8 select_select_fusion
  7.1 3.3 %all-to-all-start = ((bf16[2,96,256]{2,1,0:T(8,128)(2,1)}), bf16[2,96,256]{2,1,0:T(8,128)(2,1)S(1)}, u32[]{:S(2)}, u32[]{:S(2)}) async-start(bf16[2,96,256]{2,1,0:T(8,128)(2,1)} %select_select_fusion), calls=%async_computation | async-start | bytes 196608 | tf_op jit(solution)/shard_map/all_to_all | solution.py:342
  10.4 0.7 compare_and_fusion.1
  11.1 0.7 compare_select_fusion.1
  11.8 0.8 reduce-window.4
  12.6 0.6 slice.20
  13.2 0.6 iota_compare_fusion.8
  13.9 0.7 select_reduce_fusion
  14.7 0.6 divide_select_fusion
  15.3 0.2 fusion.19
  15.5 2.1 %gather_fusion.1 = bf16[384,256]{1,0:T(8,128)(2,1)S(1)} fusion(bf16[192,256]{1,0:T(8,128)(2,1)S(1)} %bitcast.85, s32[1024]{0:T(1024)S(1)} %pad_clamp_fusion), kind=kCustom, calls=%fused_computation.1 | custom fusion | bytes 394752 | tf_op jit(solution)/shard_map/jit(_take)/gather | solution.py:66
  17.6 0.3 fusion.11
  17.9 0.5 fusion.33
  18.4 0.3 multiply_reduce_fusion.1
  18.7 1.6 %multiply_convert_fusion.1 = (bf16[384,1024]{0,1:T(8,128)(2,1)S(1)}, f32[384,1024]{0,1:T(8,128)S(1)}) fusion(bf16[1024,1024]{1,0:T(8,128)(2,1)S(1)} %copy-done, f32[384,1024]{1,0:T(8,128)S(1)} %get-tuple-element.26, f32[384]{0:T(512)S(1)} %fusion.27, f32[384]{0:T(512)S(1)} %broadcast_multiply_fusion.1), kind=kOutput, calls=%fused_computation.12 | convolution fusion | flops 808452096 | bytes 6032384 | tf_op jit(solution)/shard_map/dot_general | solution.py:75
  20.3 0.7 multiply_convert_fusion.3
  21.1 0.3 fusion.34
  21.5 0.7 copy-done.3
  22.2 0.1 copy-done.6
  22.3 0.6 multiply_reduce_fusion.2
  22.9 0.2 fusion.20
  23.1 0.1 broadcast_add_fusion
  23.2 0.3 fusion.38
  23.5 0.7 fusion.10
  24.3 0.3 fusion.36
  24.6 0.3 fusion.37
  24.9 0.6 fusion.2
  25.5 1.2 %multiply_reduce_fusion = (f32[384]{0:T(512)S(1)}, f32[384,1024]{1,0:T(8,128)S(1)}) fusion(f32[384,1024]{1,0:T(8,128)S(1)} %get-tuple-element.26, f32[384]{0:T(512)S(1)} %broadcast_multiply_fusion.1, bf16[384,1024]{0,1:T(8,128)(2,1)S(1)} %fusion.2, bf16[1024,1024]{1,0:T(8,128)(2,1)S(1)} %copy-done), kind=kOutput, calls=%fused_computation.11 | convolution fusion | flops 806485632 | bytes 6032384 | tf_op jit(solution)/shard_map/dot_general | solution.py:85
  26.7 1.5 %multiply_convert_fusion.refs_0_ = bf16[1024,1024]{1,0:T(8,128)(2,1)S(1)} fusion(bf16[384,1024]{0,1:T(8,128)(2,1)S(1)} %fusion.2, f32[384,1024]{1,0:T(8,128)S(1)} %get-tuple-element.26, f32[384]{0:T(512)S(1)} %fusion.27, f32[384]{0:T(512)S(1)} %broadcast_multiply_fusion.1), kind=kOutput, calls=%fused_computation.3 | convolution fusion | flops 808583168 | bytes 4459520 | tf_op jit(solution)/shard_map/dot_general | solution.py:84
  28.2 0.5 fusion.31
  28.7 0.4 add_convert_fusion
  29.0 0.5 fusion.6.refs_1_
  29.5 0.4 fusion.35
  29.9 0.4 fusion.14
  30.3 0.6 fusion.23
  30.9 0.5 fusion.7.refs_2_
  31.5 53.7 %shard_map.146 = (f32[512,1024]{1,0:T(8,128)S(1)}, f32[128,1024]{1,0:T(8,128)S(1)}, f32[128,1024]{1,0:T(8,128)S(1)}, f32[16,128]{1,0:T(8,128)S(1)}, f32[2,96,256]{2,1,0:T(8,128)S(1)}) custom-call(bf16[1024,1024]{1,0:T(8,128)(2,1)S(1)} %multiply_convert_fusion.refs_0_, bf16[256,1024]{1,0:T(8,128)(2,1)S(1)} %fusion.6.refs_1_, ...), custom_call_target="tpu_custom_call" | custom-call | tf_op jit(solution)/shard_map/pallas_call | solution.py:289
  85.2 1.3 %copy-done.1 = f32[512,1024]{1,0:T(8,128)} copy-done((f32[512,1024]{1,0:T(8,128)}, f32[512,1024]{1,0:T(8,128)S(1)}, u32[]{:S(2)}) %copy-start.1) | copy-done | bytes 2097176
  86.6 2.8 %scatter_custom_fusion = f32[1536,256]{1,0:T(8,128)} fusion(s32[192]{0:T(256)S(1)} %bitcast.100, f32[192,256]{1,0:T(8,128)S(1)} %bitcast.98, f32[]{:T(128)} %constant.27.clone.1), kind=kCustom, calls=%fused_computation.40 | custom fusion | flops 49152 | bytes 1572868 | tf_op jit(solution)/shard_map/scatter-add | solution.py:387
  89.4 0.8 copy.51
  90.2 3.2 %copy.52 = f32[512,1024]{1,0:T(8,128)} copy(f32[512,1024]{1,0:T(8,128)} %copy-done.1) | data formatting | bytes 4194304
  93.4 0.8 copy.53
  94.2 0.6 copy.54
  (29 shorter events, 0.5 us)
Async XLA Ops:
  0.6 18.1 %copy-start = (bf16[1024,1024]{1,0:T(8,128)(2,1)S(1)}, bf16[1024,1024]{1,0:T(8,128)(2,1)}, u32[]{:S(2)}) copy-start(bf16[1024,1024]{1,0:T(8,128)(2,1)} %param.19) | copy-start | bytes 6291460
  4.2 13.5 %copy-start.5 = (s32[384]{0:T(512)S(1)}, s32[384]{0:T(512)}, u32[]{:S(2)}) copy-start(s32[384]{0:T(512)} %param.15) | copy-start | bytes 4612
  4.2 13.5 %copy-start.7 = (bf16[16,256]{1,0:T(8,128)(2,1)S(1)}, bf16[16,256]{1,0:T(8,128)(2,1)}, u32[]{:S(2)}) copy-start(bf16[16,256]{1,0:T(8,128)(2,1)} %param.17) | copy-start | bytes 24580
  6.3 11.6 %copy-start.2 = (bf16[256,1024]{1,0:T(8,128)(2,1)S(1)}, bf16[256,1024]{1,0:T(8,128)(2,1)}, u32[]{:S(2)}) copy-start(bf16[256,1024]{1,0:T(8,128)(2,1)} %param.18) | copy-start | bytes 1572868
  7.1 8.5 %all-to-all-start = ((bf16[2,96,256]{2,1,0:T(8,128)(2,1)}), bf16[2,96,256]{2,1,0:T(8,128)(2,1)S(1)}, u32[]{:S(2)}, u32[]{:S(2)}) async-start(bf16[2,96,256]{2,1,0:T(8,128)(2,1)} %select_select_fusion), calls=%async_computation | async-start | bytes 196608 | tf_op jit(solution)/shard_map/all_to_all | solution.py:342
  21.0 1.1 %copy-start.3 = (bf16[384,1024]{1,0:T(8,128)(2,1)S(1)}, bf16[384,1024]{1,0:T(8,128)(2,1)}, u32[]{:S(2)}) copy-start(bf16[384,1024]{1,0:T(8,128)(2,1)} %param.21) | copy-start | bytes 2359300
  21.1 1.3 %copy-start.6 = (bf16[256,1024]{1,0:T(8,128)(2,1)S(1)}, bf16[256,1024]{1,0:T(8,128)(2,1)}, u32[]{:S(2)}) copy-start(bf16[256,1024]{1,0:T(8,128)(2,1)} %param.20) | copy-start | bytes 1572868
  29.0 1.3 %copy-start.4 = (s32[384]{0:T(512)S(1)}, s32[384]{0:T(512)}, u32[]{:S(2)}) copy-start(s32[384]{0:T(512)} %param.14) | copy-start | bytes 4612
  85.2 1.4 %copy-start.1 = (f32[512,1024]{1,0:T(8,128)}, f32[512,1024]{1,0:T(8,128)S(1)}, u32[]{:S(2)}) copy-start(f32[512,1024]{1,0:T(8,128)S(1)} %get-tuple-element.46) | copy-start | bytes 6291460

commit v2 on v1

--- a/solution.py
+++ b/solution.py
@@ -19,16 +19,17 @@
 
 
 def sequence_layout(lengths, count):
-    ends = jnp.cumsum(lengths, dtype=jnp.int32)
+    kinds = jnp.arange(lengths.shape[0], dtype=jnp.int32)
+    ends = jnp.sum(
+        jnp.where(kinds[None, :] <= kinds[:, None], lengths[None, :], 0), axis=1, dtype=jnp.int32
+    )
     position = jnp.arange(count, dtype=jnp.int32)
-    live = position < ends[-1]
-    sequence = jnp.sum(
-        (position[:, None] >= ends[None, :]).astype(jnp.int32), axis=1, dtype=jnp.int32
-    )
-    chosen = sequence[:, None] == jnp.arange(lengths.shape[0], dtype=jnp.int32)[None, :]
-    row_length = jnp.sum(jnp.where(chosen, lengths[None, :], 0), axis=1, dtype=jnp.int32)
-    allowed = (sequence[:, None] == sequence[None, :]) & (position[None, :] <= position[:, None])
-    allowed = allowed & live[:, None] & live[None, :]
+    member = (position[:, None] < ends[None, :]) & (position[:, None] >= (ends - lengths)[None, :])
+    row_length = jnp.sum(jnp.where(member, lengths[None, :], 0), axis=1, dtype=jnp.int32)
+    first = jnp.sum(jnp.where(member, (ends - lengths)[None, :], 0), axis=1, dtype=jnp.int32)
+    live = row_length > 0
+    allowed = (position[None, :] >= first[:, None]) & (position[None, :] <= position[:, None])
+    allowed = allowed & live[:, None]
     safe_length = jnp.maximum(row_length, 1).astype(jnp.float32)
     inverse_length = jnp.where(live, 1.0 / safe_length, jnp.zeros_like(safe_length))
     return (allowed, inverse_length, live)
@@ -63,12 +64,13 @@
     loss_scale = count ** (-0.5)
     allowed, inverse_length, live = sequence_layout(lengths, count)
     cotangent = jnp.where(live[:, None], cotangent, jnp.zeros_like(cotangent))
-    item_rows = jnp.take(fetched, item_slot, axis=0)
+    item_hot = item_slot[:, None] == jnp.arange(fetched.shape[0], dtype=jnp.int32)[None, :]
+    item_rows = jnp.dot(item_hot.astype(jnp.bfloat16), fetched, preferred_element_type=jnp.float32)
     action_hot = action_id[:, None] == jnp.arange(action_table.shape[0], dtype=jnp.int32)[None, :]
     action_rows = jnp.dot(
         action_hot.astype(jnp.bfloat16), action_table, preferred_element_type=jnp.float32
     )
-    embedded = (item_rows.astype(jnp.float32) + action_rows).astype(jnp.bfloat16)
+    embedded = (item_rows + action_rows).astype(jnp.bfloat16)
     hidden = jnp.dot(embedded, w_in, preferred_element_type=jnp.float32)
     normed_full, norm_back = jax.vjp(layer_norm, hidden)
     normed = normed_full.astype(jnp.bfloat16)
@@ -125,22 +127,30 @@
     slot_got,
     *rest,
 ):
-    got = rest[: dp_bits + 2]
+    got = rest[:4]
     send_sem, recv_sem, gather_send, gather_recv, action_send, action_recv, slot_send, slot_recv = rest[
-        dp_bits + 2 :
+        4:12
     ]
+    line_send, line_recv, line_back_send, line_back_recv = rest[12:]
     chunks, _, rows, columns = work.shape
     table = lax.axis_index("table")
     other_table = 1 - table
     steps = [("rep", *flip("rep", 0)), ("table", *flip("table", 0))]
     steps += [("dp", *flip("dp", bit)) for bit in range(dp_bits)]
 
+    line = (1 << dp_bits) // 2
+    place_in_line = lax.axis_index("dp") // 2
+    low = lax.axis_index("dp") % 2
+
+    def line_place(offset):
+        return (place_in_line + offset) % line
+
     barrier = pltpu.get_barrier_semaphore()
-    for axis, partner, _ in steps:
-        pl.semaphore_signal(
-            barrier, inc=1, device_id={axis: partner}, device_id_type=pl.DeviceIdType.MESH
-        )
-    pl.semaphore_wait(barrier, len(steps))
+    peers = [{axis: partner} for axis, partner, _ in steps[:3]]
+    peers += [{"dp": line_place(offset) * 2 + low} for offset in range(1, line)]
+    for peer in peers:
+        pl.semaphore_signal(barrier, inc=1, device_id=peer, device_id_type=pl.DeviceIdType.MESH)
+    pl.semaphore_wait(barrier, len(peers))
 
     def remote(src, dst, send, recv, step):
         axis, partner, _ = steps[step]
@@ -155,7 +165,7 @@
 
     starts, counts = [0], [rows]
     sent = []
-    halving = [0] + list(range(2, dp_bits + 2))
+    halving = [0, 2]
     for step in halving:
         half = counts[-1] // 2
         own = steps[step][2]
@@ -184,39 +194,74 @@
         else:
             action_acc[step + 1, 0] = action_acc[step, 0] + action_got[step, 0]
 
-    def reduce_copy(chunk, step):
+    piece = counts[2] // line
+
+    def piece_at(place):
+        return pl.ds(pl.multiple_of(starts[2] + place * piece, 16), piece)
+
+    def line_copy(chunk, offset, back):
+        target = line_place(offset)
+        if back:
+            src = dst = final.at[chunk, piece_at(place_in_line)]
+            sems = line_back_send.at[chunk, offset - 1], line_back_recv.at[chunk, offset - 1]
+        else:
+            src = work.at[chunk, table, piece_at(target)]
+            dst = got[3].at[chunk, offset - 1]
+            sems = line_send.at[chunk, offset - 1], line_recv.at[chunk, offset - 1]
+        return pltpu.make_async_remote_copy(
+            src_ref=src,
+            dst_ref=dst,
+            send_sem=sems[0],
+            recv_sem=sems[1],
+            device_id={"dp": target * 2 + low},
+            device_id_type=pl.DeviceIdType.MESH,
+        )
+
+    offsets = sorted(range(1, line), key=lambda offset: -min(offset, line - offset))
+
+    def reduce_copies(chunk, step):
         if step == 0:
             src = work.at[chunk, :, pl.ds(sent[0], counts[1])]
         elif step == 1:
             src = work.at[chunk, other_table, pl.ds(starts[1], counts[1])]
+        elif step == 2:
+            src = work.at[chunk, table, pl.ds(sent[1], counts[2])]
         else:
-            src = work.at[chunk, table, pl.ds(sent[step - 1], counts[step])]
-        return remote(
-            src, got[step].at[chunk], send_sem.at[chunk, step], recv_sem.at[chunk, step], step
-        )
+            return [line_copy(chunk, offset, False) for offset in offsets]
+        sems = send_sem.at[chunk, step], recv_sem.at[chunk, step]
+        return [remote(src, got[step].at[chunk], *sems, step)]
 
     def reduce_add(chunk, step):
-        part = max(step, 1)
         if step == 0:
             at = (chunk, slice(None), pl.ds(starts[1], counts[1]))
+        elif step < 3:
+            at = (chunk, table, pl.ds(starts[step], counts[step]))
         else:
-            at = (chunk, table, pl.ds(starts[part], counts[part]))
+            total = work[chunk, table, piece_at(place_in_line)].astype(jnp.float32)
+            for offset in range(1, line):
+                total += got[3][chunk, offset - 1].astype(jnp.float32)
+            final[chunk, piece_at(place_in_line)] = total.astype(jnp.bfloat16)
+            return
         total = work[at].astype(jnp.float32) + got[step][chunk].astype(jnp.float32)
-        if step == dp_bits + 1:
-            final[chunk, pl.ds(starts[part], counts[part])] = total.astype(jnp.bfloat16)
-        else:
-            work[at] = total.astype(jnp.bfloat16)
-
-    backward = list(reversed(range(len(halving))))
-
-    def gather_copy(chunk, place):
-        at = backward[place]
-        piece = final.at[chunk, pl.ds(starts[at + 1], counts[at + 1])]
-        return remote(
-            piece, piece, gather_send.at[chunk, place], gather_recv.at[chunk, place], halving[at]
-        )
-
-    reduces, gathers = len(steps), len(backward)
+        work[at] = total.astype(jnp.bfloat16)
+
+    def gather_copies(chunk, place):
+        if place == 0:
+            return [line_copy(chunk, offset, True) for offset in offsets]
+        at = 2 - place
+        part = final.at[chunk, pl.ds(starts[at + 1], counts[at + 1])]
+        sems = gather_send.at[chunk, place - 1], gather_recv.at[chunk, place - 1]
+        return [remote(part, part, *sems, halving[at])]
+
+    def start(copies):
+        for copy in copies:
+            copy.start()
+
+    def received(copies):
+        for copy in copies:
+            copy.wait_recv()
+
+    reduces, gathers, action_steps = 4, 3, len(steps)
     half_proj, half_in, half_out = proj_ref.shape[0] // 2, in_ref.shape[0] // 2, out_ref.shape[0] // 2
     for chunk in range(chunks):
         wide = slice(chunk * columns, (chunk + 1) * columns)
@@ -228,7 +273,7 @@
             work[chunk, side, half_proj + half_in :] = out_ref[
                 side * half_out : (side + 1) * half_out, wide
             ]
-        reduce_copy(chunk, 0).start()
+        start(reduce_copies(chunk, 0))
     action_copy(0).start()
 
     for wave in range(chunks + reduces + gathers - 1):
@@ -237,40 +282,42 @@
             if at < 0 or at >= reduces + gathers:
                 continue
             if at < reduces:
-                reduce_copy(chunk, at).wait_recv()
+                received(reduce_copies(chunk, at))
                 reduce_add(chunk, at)
                 if at + 1 < reduces:
-                    reduce_copy(chunk, at + 1).start()
+                    start(reduce_copies(chunk, at + 1))
                 else:
-                    gather_copy(chunk, 0).start()
+                    start(gather_copies(chunk, 0))
             else:
                 place = at - reduces
-                gather_copy(chunk, place).wait_recv()
+                received(gather_copies(chunk, place))
                 if place + 1 < gathers:
-                    gather_copy(chunk, place + 1).start()
+                    start(gather_copies(chunk, place + 1))
                 else:
                     wide = slice(chunk * columns, (chunk + 1) * columns)
-                    proj_o[:, wide] = final[chunk, :half_proj].astype(jnp.float32)
-                    in_o[:, wide] = final[chunk, half_proj : half_proj + half_in].astype(jnp.float32)
-                    out_o[:, wide] = final[chunk, half_proj + half_in :].astype(jnp.float32)
-        if wave < reduces:
+                    proj_o[:, wide] = final[chunk, :half_proj]
+                    in_o[:, wide] = final[chunk, half_proj : half_proj + half_in]
+                    out_o[:, wide] = final[chunk, half_proj + half_in :]
+        if wave < action_steps:
             action_copy(wave).wait_recv()
             action_add(wave)
-            if wave + 1 < reduces:
+            if wave + 1 < action_steps:
                 action_copy(wave + 1).start()
 
-    action_o[...] = action_acc[reduces, 0]
+    action_o[...] = action_acc[action_steps, 0]
     slot_copy.wait_recv()
     slot_o[table] = slot_ref[table]
     slot_o[other_table] = slot_got[...]
     slot_copy.wait_send()
-    for step in range(reduces):
+    for step in range(action_steps):
         action_copy(step).wait_send()
-        for chunk in range(chunks):
-            reduce_copy(chunk, step).wait_send()
-    for place in range(gathers):
-        for chunk in range(chunks):
-            gather_copy(chunk, place).wait_send()
+    for chunk in range(chunks):
+        for step in range(reduces):
+            for copy in reduce_copies(chunk, step):
+                copy.wait_send()
+        for place in range(gathers):
+            for copy in gather_copies(chunk, place):
+                copy.wait_send()
 
 
 def combine(grad_proj, grad_in, grad_out, action_parts, slot_parts, dp_bits):
@@ -281,17 +328,17 @@
     _, actions, action_wide = action_parts.shape
     got = [pltpu.VMEM((CHUNKS, 2, rows // 2, columns), jnp.bfloat16)]
     got += [pltpu.VMEM((CHUNKS, rows // 2, columns), jnp.bfloat16)]
-    got += [
-        pltpu.VMEM((CHUNKS, rows >> (bit + 2), columns), jnp.bfloat16) for bit in range(dp_bits)
-    ]
+    got += [pltpu.VMEM((CHUNKS, rows // 4, columns), jnp.bfloat16)]
+    line = (1 << dp_bits) // 2
+    got += [pltpu.VMEM((CHUNKS, line - 1, rows // 4 // line, columns), jnp.bfloat16)]
     dma = pltpu.SemaphoreType.DMA
     vmem = pl.BlockSpec(memory_space=pltpu.VMEM)
     return pl.pallas_call(
         lambda *refs: combine_kernel(dp_bits, *refs),
         out_shape=(
-            jax.ShapeDtypeStruct((grad_proj.shape[0] // 2, wide), jnp.float32),
-            jax.ShapeDtypeStruct((grad_in.shape[0] // 2, wide), jnp.float32),
-            jax.ShapeDtypeStruct((grad_out.shape[0] // 2, wide), jnp.float32),
+            jax.ShapeDtypeStruct((grad_proj.shape[0] // 2, wide), jnp.bfloat16),
+            jax.ShapeDtypeStruct((grad_in.shape[0] // 2, wide), jnp.bfloat16),
+            jax.ShapeDtypeStruct((grad_out.shape[0] // 2, wide), jnp.bfloat16),
             jax.ShapeDtypeStruct((actions, action_wide), jnp.float32),
             jax.ShapeDtypeStruct(slot_parts.shape, jnp.float32),
         ),
@@ -304,14 +351,15 @@
             pltpu.VMEM((steps, 2, actions, action_wide), jnp.float32),
             pltpu.VMEM(slot_parts.shape[1:], jnp.float32),
             *got,
-            dma((CHUNKS, steps)),
-            dma((CHUNKS, steps)),
-            dma((CHUNKS, steps - 1)),
-            dma((CHUNKS, steps - 1)),
+            dma((CHUNKS, 3)),
+            dma((CHUNKS, 3)),
+            dma((CHUNKS, 2)),
+            dma((CHUNKS, 2)),
             dma((steps,)),
             dma((steps,)),
             dma,
             dma,
+            *[dma((CHUNKS, line - 1))] * 4,
         ],
         compiler_params=pltpu.CompilerParams(
             collective_id=0, has_side_effects=True, vmem_limit_bytes=40 * 2**20
@@ -337,11 +385,22 @@
     slot_count = fetched_count // table_count
     width = item_table.shape[1]
     valid = jnp.arange(slot_count, dtype=jnp.int32)[None, :] < fetch_count[0][:, None]
-    taken = jnp.take(item_table, fetch_rows[0], axis=0).reshape(table_count, slot_count, width)
-    outgoing = jnp.where(valid[:, :, None], taken, jnp.zeros_like(taken))
-    fetched = lax.all_to_all(outgoing, "table", split_axis=0, concat_axis=0, tiled=True).reshape(
-        fetched_count, width
-    )
+    rows_at = jnp.arange(item_table.shape[0], dtype=jnp.int32)
+    fetch_hot = (fetch_rows[0][:, None] == rows_at[None, :]) & valid.reshape(fetched_count, 1)
+    outgoing = jnp.dot(
+        fetch_hot.astype(jnp.bfloat16), item_table, preferred_element_type=jnp.float32
+    ).astype(jnp.bfloat16)
+    outgoing = outgoing.reshape(table_count, slot_count, width)
+    if table_count == 2:
+        first = lax.axis_index("table") == 0
+        own = jnp.where(first, outgoing[0], outgoing[1])
+        asked = jnp.where(first, outgoing[1], outgoing[0])
+        came = lax.ppermute(asked, "table", [(0, 1), (1, 0)])
+        fetched = jnp.concatenate([jnp.where(first, own, came), jnp.where(first, came, own)])
+    else:
+        fetched = lax.all_to_all(outgoing, "table", split_axis=0, concat_axis=0, tiled=True).reshape(
+            fetched_count, width
+        )
     dense, slot_grad = local_terms(
         fetched, item_slot, action_id, lengths[0], action_table, w_in, w_proj, w_out, cotangent
     )
@@ -354,6 +413,7 @@
     dp_bits = dp_count.bit_length() - 1
     rows = (grad_in.shape[0] + grad_proj.shape[0] + grad_out.shape[0]) // 2
     pairs = table_count == 2 and lax.axis_size("rep") == 2 and dp_count == 1 << dp_bits
+    pairs = pairs and dp_bits > 1
     if pairs and rows % (16 << (dp_bits + 1)) == 0:
         actions = action_grad.shape[0]
         proj_total, in_total, out_total, action_total, returned = combine(
@@ -364,7 +424,12 @@
             slot_grad.reshape(table_count, slot_count, width),
             dp_bits,
         )
-        totals = (in_total, proj_total, out_total, action_total)
+        totals = (
+            in_total.astype(jnp.float32),
+            proj_total.astype(jnp.float32),
+            out_total.astype(jnp.float32),
+            action_total,
+        )
     else:
         returned = lax.all_to_all(
             slot_grad.reshape(table_count, slot_count, width),
@@ -380,11 +445,10 @@
             lax.psum_scatter(action_grad, "table", scatter_dimension=1, tiled=True),
         )
         totals = lax.psum((shares[0], shares[1], shares[2], shares[3]), ("dp", "rep"))
-    returned = jnp.where(valid[:, :, None], returned, jnp.zeros_like(returned))
-    item_grad = (
-        jnp.zeros((item_table.shape[0], width), jnp.float32)
-        .at[fetch_rows[0]]
-        .add(returned.reshape(fetched_count, width))
+    item_grad = jnp.dot(
+        fetch_hot.astype(jnp.float32).T,
+        returned.reshape(fetched_count, width),
+        precision=lax.Precision.HIGHEST,
     )
     return (item_grad, totals[0], totals[1], totals[2], totals[3])
 

time: 95.2 us -> 77.4 us (0.81)
  local copies, waits for them, and re-layouts: 13 us -> 1.63 us
  other arithmetic: 13.3 us -> 6.75 us
  matrix products: 10.5 us -> 15 us
  Pallas kernels: 53.7 us -> 50 us
  starting transfers between devices: 3.34 us -> 2.11 us
    unnamed x21 -> x19, local copies, waits for them, and re-layouts: 8.07 us -> 1.47 us
    dot_general x0 -> x3, matrix products: none -> 4.51 us  [the longest x1 2.64 us: shards(): jnp.dot(fetch_hot.astype(jnp.float32).T, returned.reshape(fetched_count,...]
    gather x2 -> x0, local copies, waits for them, and re-layouts: 4.18 us -> none  [the longest x1 2.12 us: shards(): jnp.take(item_table, fetch_rows[0], axis=0)]
    pallas_call x1, Pallas kernels: 53.7 us -> 50 us  [combine(): pl.pallas_call(lambda *refs: combine_kernel(dp_bits, *refs), out_shape=(j...]
    all_to_all x1 -> x0, starting transfers between devices: 3.34 us -> none  [shards(): lax.all_to_all(outgoing, 'table', split_axis=0, concat_axis=0, tiled=True)]
    convert_element_type x0 -> x3, other arithmetic: none -> 3.25 us  [the longest x1 1.56 us: shards(): proj_total.astype(jnp.float32)]
    scatter-add x1 -> x0, other arithmetic: 2.8 us -> none  [shards(): item_grad = jnp.zeros((item_table.shape[0], width), jnp.float32).at[fetch...]
    select_n x4 -> x2, other arithmetic: 2.37 us -> 0.02 us  [the longest x1 0.01 us: shards(): jnp.where(first, own, came)]
  transfers between devices with their start and end apart: 1 -> 1, of which waited for: 0 -> 1; matrix products, arithmetic and copies ran while one was open for 5% -> 1% of each run, Pallas kernels for 0% -> 0%
where the time goes in v2:
time: 77.4 us; the launch traced here: 77.3 us
  Pallas kernels  50 us (65%)
  matrix products  15 us (19%)
  other arithmetic  6.75 us (9%)
  starting transfers between devices  2.11 us (3%)
  local copies, waits for them, and re-layouts  1.63 us (2%)
  between operations  0.96 us (1%)
    pallas_call x1, Pallas kernels, combine(): pl.pallas_call(lambda *refs: combine_kernel(dp_bits, *refs), out_shape=(j...  50 us
    dot_general x1, matrix products, shards(): jnp.dot(fetch_hot.astype(jnp.float32).T, returned.reshape(fetched_count,...  2.64 us
    ppermute x1, starting transfers between devices, shards(): came = lax.ppermute(asked, 'table', [(0, 1), (1, 0)])  2.11 us
    dot_general x1, matrix products, shards(): jnp.dot(fetch_hot.astype(jnp.bfloat16), item_table, preferred_element_typ...  1.62 us
    convert_element_type x1, other arithmetic, shards(): proj_total.astype(jnp.float32)  1.56 us
    dot_general x1, matrix products, local_terms(): projected = jnp.dot(normed, w_proj, preferred_element_type=jnp.float32)  1.56 us
  transfers between devices with their start and end apart: 1, of which 1 were waited for; matrix products, arithmetic and copies ran while one was open for 1% of the time, Pallas kernels for 0%

profile of v2, /device:TPU:1, one launch (start us, length us, event | category | flops | bytes accessed | tf_op | source)
XLA Modules:
  0.0 77.3 jit_solution(12112073639865053876)
XLA Ops:
  0.6 0.0 copy-start
  0.6 0.0 copy-start.7
  0.7 0.9 %iota_compare_fusion.12 = pred[2,96]{1,0:T(4,128)(4,1)S(1)} fusion(s32[2]{0:T(128)} %bitcast.102), kind=kLoop, calls=%fused_computation.97 | loop fusion | flops 192 | bytes 200 | tf_op jit(solution)/shard_map/lt | solution.py:387
  1.6 0.1 lt.41
  1.7 1.6 %fusion.19 = bf16[192,256]{1,0:T(8,128)(2,1)S(1)} fusion(bf16[1536,256]{1,0:T(8,128)(2,1)} %param.11, s32[192]{0:T(256)} %bitcast.98, pred[192]{0:T(512)(128)(4,1)S(1)} %lt.41), kind=kOutput, calls=%fused_computation.39 | convolution fusion | flops 151633920 | bytes 885696 | tf_op jit(solution)/shard_map/dot_general | solution.py:390
  3.3 2.1 %collective-permute-start = (bf16[96,256]{1,0:T(8,128)(2,1)S(1)}, bf16[96,256]{1,0:T(8,128)(2,1)S(1)}, u32[]{:S(2)}, u32[]{:S(2)}) collective-permute-start(bf16[96,256]{1,0:T(8,128)(2,1)S(1)} %broadcast_select_fusion.3), channel_id=1, source_target_pairs={{0,2},{2,0},{1,3},{3,1},{4,6},{6,4},{5,7},{7,5},{8,10},{10,8},{9,1... | collective-permute-start | bytes 147464 | tf_op jit(solution)/shard_map/ppermute | solution.py:398
  5.4 0.0 copy-done.7
  5.4 0.1 select_reduce_fusion.2
  5.5 0.1 select_reduce_fusion.1
  5.6 0.2 fusion.28
  5.8 0.3 fusion.33
  6.1 0.8 %collective-permute-done = bf16[96,256]{1,0:T(8,128)(2,1)S(1)} collective-permute-done((bf16[96,256]{1,0:T(8,128)(2,1)S(1)}, bf16[96,256]{1,0:T(8,128)(2,1)S(1)}, u32[]{:S(2)}, u32[]{:S(2)}) %collective-permute-start) | collective-permute-done | bytes 49184 | tf_op jit(solution)/shard_map/ppermute | solution.py:398
  6.9 0.3 fusion.16
  7.2 0.5 fusion.50
  7.6 0.3 multiply_reduce_fusion.1
  8.0 1.6 %multiply_convert_fusion.1 = (bf16[384,1024]{0,1:T(8,128)(2,1)S(1)}, f32[384,1024]{0,1:T(8,128)S(1)}) fusion(bf16[1024,1024]{1,0:T(8,128)(2,1)S(1)} %copy-done, f32[384,1024]{1,0:T(8,128)S(1)} %get-tuple-element.30, f32[384]{0:T(512)S(1)} %fusion.42, f32[384]{0:T(512)S(1)} %broadcast_multiply_fusion.1), kind=kOutput, calls=%fused_computation.9 | convolution fusion | flops 808452096 | bytes 6032384 | tf_op jit(solution)/shard_map/dot_general | solution.py:77
  9.5 0.1 fusion.49
  9.6 0.7 multiply_convert_fusion.3
  10.3 0.0 copy-start.2
  10.3 0.0 copy-start.8
  10.3 0.3 fusion.51
  10.7 0.1 fusion.31
  10.8 0.7 copy-done.2
  11.5 0.1 copy-done.8
  11.6 0.6 multiply_reduce_fusion.2
  12.2 0.2 fusion.29
  12.4 0.1 broadcast_add_fusion
  12.5 0.3 fusion.55
  12.8 0.8 fusion.10
  13.5 0.3 fusion.53
  13.9 0.3 fusion.54
  14.2 0.6 fusion.2
  14.8 1.2 %multiply_reduce_fusion = (f32[384]{0:T(512)S(1)}, f32[384,1024]{1,0:T(8,128)S(1)}) fusion(f32[384,1024]{1,0:T(8,128)S(1)} %get-tuple-element.30, f32[384]{0:T(512)S(1)} %broadcast_multiply_fusion.1, bf16[384,1024]{0,1:T(8,128)(2,1)S(1)} %fusion.2, bf16[1024,1024]{1,0:T(8,128)(2,1)S(1)} %copy-done), kind=kOutput, calls=%fused_computation.8 | convolution fusion | flops 806485632 | bytes 6032384 | tf_op jit(solution)/shard_map/dot_general | solution.py:87
  16.0 1.5 %multiply_convert_fusion.refs_0_ = bf16[1024,1024]{1,0:T(8,128)(2,1)S(1)} fusion(bf16[384,1024]{0,1:T(8,128)(2,1)S(1)} %fusion.2, f32[384,1024]{1,0:T(8,128)S(1)} %get-tuple-element.30, f32[384]{0:T(512)S(1)} %fusion.42, f32[384]{0:T(512)S(1)} %broadcast_multiply_fusion.1), kind=kOutput, calls=%fused_computation | convolution fusion | flops 808583168 | bytes 4459520 | tf_op jit(solution)/shard_map/dot_general | solution.py:86
  17.5 0.5 fusion.48
  18.0 0.4 add_convert_fusion
  18.3 0.5 fusion.6.refs_1_
  18.8 0.4 fusion.52
  19.2 0.4 fusion.22
  19.6 0.6 fusion.32
  20.2 0.5 fusion.7.refs_2_
  20.7 50.0 %shard_map.146 = (bf16[512,1024]{1,0:T(8,128)(2,1)S(1)}, bf16[128,1024]{1,0:T(8,128)(2,1)S(1)}, bf16[128,1024]{1,0:T(8,128)(2,1)S(1)}, f32[16,128]{1,0:T(8,128)S(1)}, f32[2,96,256]{2,1,0:T(8,128)S(1)}) custom-call(bf16[1024,1024]{1,0:T(8,128)(2,1)S(1)} %multiply_convert_fusion.refs_0_, bf16[256,1024]{1,0:T(8,128)(2,1)S(1)} %fusion.6.refs_1_, ...), custom_call_target="tpu_custom_call" | custom-call | tf_op jit(solution)/shard_map/pallas_call | solution.py:336
  70.7 0.0 copy-start.6
  70.8 0.8 %convert_element_type.138 = f32[128,1024]{1,0:T(8,128)} convert(bf16[128,1024]{1,0:T(8,128)(2,1)S(1)} %get-tuple-element.11) | non-fusion elementwise | flops 131072 | bytes 786432 | tf_op jit(solution)/shard_map/convert_element_type | solution.py:428
  71.6 0.8 %convert_element_type.140 = f32[128,1024]{1,0:T(8,128)} convert(bf16[128,1024]{1,0:T(8,128)(2,1)S(1)} %get-tuple-element.13) | non-fusion elementwise | flops 131072 | bytes 786432 | tf_op jit(solution)/shard_map/convert_element_type | solution.py:430
  72.4 2.6 %fusion.12 = f32[1536,256]{1,0:T(8,128)} fusion(f32[192,256]{1,0:T(8,128)S(1)} %bitcast.85, s32[192]{0:T(256)S(1)} %bitcast.99, pred[192]{0:T(512)(128)(4,1)S(1)} %lt.41), kind=kOutput, calls=%fused_computation.31 | convolution fusion | flops 906559488 | bytes 1770432 | tf_op jit(solution)/shard_map/dot_general | solution.py:448
  75.1 1.6 %convert_element_type.139 = f32[512,1024]{1,0:T(8,128)} convert(bf16[512,1024]{1,0:T(8,128)(2,1)S(1)} %get-tuple-element.12) | non-fusion elementwise | flops 524288 | bytes 3145728 | tf_op jit(solution)/shard_map/convert_element_type | solution.py:429
  76.7 0.6 copy.48
  (23 shorter events, 0.1 us)
Async XLA Ops:
  0.6 7.3 %copy-start = (bf16[1024,1024]{1,0:T(8,128)(2,1)S(1)}, bf16[1024,1024]{1,0:T(8,128)(2,1)}, u32[]{:S(2)}) copy-start(bf16[1024,1024]{1,0:T(8,128)(2,1)} %param.19) | copy-start | bytes 6291460
  0.6 4.8 %copy-start.7 = (s32[1,8]{1,0:T(1,128)S(1)}, s32[1,8]{1,0:T(1,128)}, u32[]{:S(2)}) copy-start(s32[1,8]{1,0:T(1,128)} %param.16) | copy-start | bytes 100
  0.7 5.2 %copy-start.3 = (s32[384]{0:T(512)S(1)}, s32[384]{0:T(512)}, u32[]{:S(2)}) copy-start(s32[384]{0:T(512)} %param.15) | copy-start | bytes 4612
  0.7 5.2 %copy-start.5 = (bf16[16,256]{1,0:T(8,128)(2,1)S(1)}, bf16[16,256]{1,0:T(8,128)(2,1)}, u32[]{:S(2)}) copy-start(bf16[16,256]{1,0:T(8,128)(2,1)} %param.17) | copy-start | bytes 24580
  0.7 6.2 %copy-start.4 = (s32[384]{0:T(512)S(1)}, s32[384]{0:T(512)}, u32[]{:S(2)}) copy-start(s32[384]{0:T(512)} %param.14) | copy-start | bytes 4612
  1.6 5.5 %copy-start.1 = (bf16[256,1024]{1,0:T(8,128)(2,1)S(1)}, bf16[256,1024]{1,0:T(8,128)(2,1)}, u32[]{:S(2)}) copy-start(bf16[256,1024]{1,0:T(8,128)(2,1)} %param.18) | copy-start | bytes 1572868
  3.3 3.6 %collective-permute-start = (bf16[96,256]{1,0:T(8,128)(2,1)S(1)}, bf16[96,256]{1,0:T(8,128)(2,1)S(1)}, u32[]{:S(2)}, u32[]{:S(2)}) collective-permute-start(bf16[96,256]{1,0:T(8,128)(2,1)S(1)} %broadcast_select_fusion.3), channel_id=1, source_target_pairs={{0,2},{2,0},{1,3},{3,1},{4,6},{6,4},{5,7},{7,5},{8,10},{10,8},{9,1... | collective-permute-start | bytes 147464 | tf_op jit(solution)/shard_map/ppermute | solution.py:398
  10.3 1.1 %copy-start.2 = (bf16[384,1024]{1,0:T(8,128)(2,1)S(1)}, bf16[384,1024]{1,0:T(8,128)(2,1)}, u32[]{:S(2)}) copy-start(bf16[384,1024]{1,0:T(8,128)(2,1)} %param.21) | copy-start | bytes 2359300
  10.3 1.3 %copy-start.8 = (bf16[256,1024]{1,0:T(8,128)(2,1)S(1)}, bf16[256,1024]{1,0:T(8,128)(2,1)}, u32[]{:S(2)}) copy-start(bf16[256,1024]{1,0:T(8,128)(2,1)} %param.20) | copy-start | bytes 1572868
  70.7 1.7 %copy-start.6 = (s32[1,192]{1,0:T(1,128)S(1)}, s32[1,192]{1,0:T(1,128)}, u32[]{:S(2)}) copy-start(s32[1,192]{1,0:T(1,128)} %param.12) | copy-start | bytes 2308

commit v3 on v2

--- a/solution.py
+++ b/solution.py
@@ -93,9 +93,9 @@
     slot_hot = (
         item_slot[:, None] == jnp.arange(fetched.shape[0], dtype=jnp.int32)[None, :]
     ).astype(jnp.float32)
-    slot_grad = jnp.dot(slot_hot.T, grad_embedded, precision=lax.Precision.HIGHEST)
+    slot_grad = jnp.dot(slot_hot.T, grad_embedded, precision=lax.Precision.HIGH)
     action_grad = jnp.dot(
-        action_hot.astype(jnp.float32).T, grad_embedded, precision=lax.Precision.HIGHEST
+        action_hot.astype(jnp.float32).T, grad_embedded, precision=lax.Precision.HIGH
     )
     return ((grad_in, grad_proj, grad_out, action_grad), slot_grad)
 
@@ -448,7 +448,7 @@
     item_grad = jnp.dot(
         fetch_hot.astype(jnp.float32).T,
         returned.reshape(fetched_count, width),
-        precision=lax.Precision.HIGHEST,
+        precision=lax.Precision.HIGH,
     )
     return (item_grad, totals[0], totals[1], totals[2], totals[3])
 

time: 77.4 us -> 76.9 us (level)
  no operation moved by 1% of the time
where the time goes in v3:
time: 76.9 us; the launch traced here: 76.7 us
  Pallas kernels  50.1 us (65%)
  matrix products  14.4 us (19%)
  other arithmetic  6.75 us (9%)
  starting transfers between devices  2.11 us (3%)
  local copies, waits for them, and re-layouts  1.63 us (2%)
  between operations  0.96 us (1%)
  waiting for transfers between devices  0.77 us (1%)
    pallas_call x1, Pallas kernels, combine(): pl.pallas_call(lambda *refs: combine_kernel(dp_bits, *refs), out_shape=(j...  50.1 us
    dot_general x1, matrix products, shards(): jnp.dot(fetch_hot.astype(jnp.float32).T, returned.reshape(fetched_count,...  2.23 us
    ppermute x1, starting transfers between devices, shards(): came = lax.ppermute(asked, 'table', [(0, 1), (1, 0)])  2.11 us
    dot_general x1, matrix products, shards(): jnp.dot(fetch_hot.astype(jnp.bfloat16), item_table, preferred_element_typ...  1.62 us
    convert_element_type x1, other arithmetic, shards(): proj_total.astype(jnp.float32)  1.56 us
    dot_general x1, matrix products, local_terms(): projected = jnp.dot(normed, w_proj, preferred_element_type=jnp.float32)  1.56 us
  transfers between devices with their start and end apart: 1, of which 1 were waited for; matrix products, arithmetic and copies ran while one was open for 1% of the time, Pallas kernels for 0%

profile of v3, /device:TPU:1, one launch (start us, length us, event | category | flops | bytes accessed | tf_op | source)
XLA Modules:
  0.0 76.7 jit_solution(8618628598195439356)
XLA Ops:
  0.6 0.0 copy-start
  0.7 0.9 %iota_compare_fusion.12 = pred[2,96]{1,0:T(4,128)(4,1)S(1)} fusion(s32[2]{0:T(128)} %bitcast.102), kind=kLoop, calls=%fused_computation.97 | loop fusion | flops 192 | bytes 200 | tf_op jit(solution)/shard_map/lt | solution.py:387
  1.6 0.1 lt.41
  1.7 1.6 %fusion.19 = bf16[192,256]{1,0:T(8,128)(2,1)S(1)} fusion(bf16[1536,256]{1,0:T(8,128)(2,1)} %param.11, s32[192]{0:T(256)} %bitcast.98, pred[192]{0:T(512)(128)(4,1)S(1)} %lt.41), kind=kOutput, calls=%fused_computation.39 | convolution fusion | flops 151633920 | bytes 885696 | tf_op jit(solution)/shard_map/dot_general | solution.py:390
  3.3 2.1 %collective-permute-start = (bf16[96,256]{1,0:T(8,128)(2,1)S(1)}, bf16[96,256]{1,0:T(8,128)(2,1)S(1)}, u32[]{:S(2)}, u32[]{:S(2)}) collective-permute-start(bf16[96,256]{1,0:T(8,128)(2,1)S(1)} %broadcast_select_fusion.3), channel_id=1, source_target_pairs={{0,2},{2,0},{1,3},{3,1},{4,6},{6,4},{5,7},{7,5},{8,10},{10,8},{9,1... | collective-permute-start | bytes 147464 | tf_op jit(solution)/shard_map/ppermute | solution.py:398
  5.4 0.1 select_reduce_fusion.2
  5.5 0.1 select_reduce_fusion.1
  5.6 0.2 fusion.28
  5.8 0.0 copy-done.3
  5.8 0.0 copy-done.5
  5.8 0.3 fusion.33
  6.1 0.8 %collective-permute-done = bf16[96,256]{1,0:T(8,128)(2,1)S(1)} collective-permute-done((bf16[96,256]{1,0:T(8,128)(2,1)S(1)}, bf16[96,256]{1,0:T(8,128)(2,1)S(1)}, u32[]{:S(2)}, u32[]{:S(2)}) %collective-permute-start) | collective-permute-done | bytes 49184 | tf_op jit(solution)/shard_map/ppermute | solution.py:398
  6.9 0.3 fusion.16
  7.2 0.5 fusion.50
  7.6 0.3 multiply_reduce_fusion.1
  8.0 1.6 %multiply_convert_fusion.1 = (bf16[384,1024]{0,1:T(8,128)(2,1)S(1)}, f32[384,1024]{0,1:T(8,128)S(1)}) fusion(bf16[1024,1024]{1,0:T(8,128)(2,1)S(1)} %copy-done, f32[384,1024]{1,0:T(8,128)S(1)} %get-tuple-element.30, f32[384]{0:T(512)S(1)} %fusion.42, f32[384]{0:T(512)S(1)} %broadcast_multiply_fusion.1), kind=kOutput, calls=%fused_computation.9 | convolution fusion | flops 808452096 | bytes 6032384 | tf_op jit(solution)/shard_map/dot_general | solution.py:77
  9.5 0.1 fusion.49
  9.6 0.7 multiply_convert_fusion.3
  10.3 0.0 copy-start.2
  10.3 0.0 copy-start.8
  10.3 0.3 fusion.51
  10.7 0.1 fusion.31
  10.8 0.7 copy-done.2
  11.5 0.1 copy-done.8
  11.6 0.6 multiply_reduce_fusion.2
  12.2 0.2 fusion.29
  12.4 0.1 broadcast_add_fusion
  12.5 0.3 fusion.55
  12.8 0.8 fusion.10
  13.5 0.3 fusion.53
  13.9 0.3 fusion.54
  14.2 0.6 fusion.2
  14.8 1.2 %multiply_reduce_fusion = (f32[384]{0:T(512)S(1)}, f32[384,1024]{1,0:T(8,128)S(1)}) fusion(f32[384,1024]{1,0:T(8,128)S(1)} %get-tuple-element.30, f32[384]{0:T(512)S(1)} %broadcast_multiply_fusion.1, bf16[384,1024]{0,1:T(8,128)(2,1)S(1)} %fusion.2, bf16[1024,1024]{1,0:T(8,128)(2,1)S(1)} %copy-done), kind=kOutput, calls=%fused_computation.8 | convolution fusion | flops 806485632 | bytes 6032384 | tf_op jit(solution)/shard_map/dot_general | solution.py:87
  16.0 1.5 %multiply_convert_fusion.refs_0_ = bf16[1024,1024]{1,0:T(8,128)(2,1)S(1)} fusion(bf16[384,1024]{0,1:T(8,128)(2,1)S(1)} %fusion.2, f32[384,1024]{1,0:T(8,128)S(1)} %get-tuple-element.30, f32[384]{0:T(512)S(1)} %fusion.42, f32[384]{0:T(512)S(1)} %broadcast_multiply_fusion.1), kind=kOutput, calls=%fused_computation | convolution fusion | flops 808583168 | bytes 4459520 | tf_op jit(solution)/shard_map/dot_general | solution.py:86
  17.5 0.5 fusion.48
  18.0 0.4 add_convert_fusion
  18.3 0.5 fusion.6.refs_1_
  18.8 0.4 fusion.52
  19.2 0.3 fusion.22
  19.5 0.5 fusion.32
  20.0 0.5 fusion.7.refs_2_
  20.5 50.1 %shard_map.146 = (bf16[512,1024]{1,0:T(8,128)(2,1)S(1)}, bf16[128,1024]{1,0:T(8,128)(2,1)S(1)}, bf16[128,1024]{1,0:T(8,128)(2,1)S(1)}, f32[16,128]{1,0:T(8,128)S(1)}, f32[2,96,256]{2,1,0:T(8,128)S(1)}) custom-call(bf16[1024,1024]{1,0:T(8,128)(2,1)S(1)} %multiply_convert_fusion.refs_0_, bf16[256,1024]{1,0:T(8,128)(2,1)S(1)} %fusion.6.refs_1_, ...), custom_call_target="tpu_custom_call" | custom-call | tf_op jit(solution)/shard_map/pallas_call | solution.py:336
  70.6 0.0 copy-start.6
  70.7 0.8 %convert_element_type.138 = f32[128,1024]{1,0:T(8,128)} convert(bf16[128,1024]{1,0:T(8,128)(2,1)S(1)} %get-tuple-element.11) | non-fusion elementwise | flops 131072 | bytes 786432 | tf_op jit(solution)/shard_map/convert_element_type | solution.py:428
  71.5 0.8 %convert_element_type.140 = f32[128,1024]{1,0:T(8,128)} convert(bf16[128,1024]{1,0:T(8,128)(2,1)S(1)} %get-tuple-element.13) | non-fusion elementwise | flops 131072 | bytes 786432 | tf_op jit(solution)/shard_map/convert_element_type | solution.py:430
  72.3 2.2 %fusion.12 = f32[1536,256]{1,0:T(8,128)} fusion(f32[192,256]{1,0:T(8,128)S(1)} %bitcast.85, s32[192]{0:T(256)S(1)} %bitcast.99, pred[192]{0:T(512)(128)(4,1)S(1)} %lt.41), kind=kOutput, calls=%fused_computation.31 | convolution fusion | flops 453574656 | bytes 1770432 | tf_op jit(solution)/shard_map/dot_general | solution.py:448
  74.6 1.6 %convert_element_type.139 = f32[512,1024]{1,0:T(8,128)} convert(bf16[512,1024]{1,0:T(8,128)(2,1)S(1)} %get-tuple-element.12) | non-fusion elementwise | flops 524288 | bytes 3145728 | tf_op jit(solution)/shard_map/convert_element_type | solution.py:429
  76.1 0.6 copy.48
  (23 shorter events, 0.1 us)
Async XLA Ops:
  0.6 7.3 %copy-start = (bf16[1024,1024]{1,0:T(8,128)(2,1)S(1)}, bf16[1024,1024]{1,0:T(8,128)(2,1)}, u32[]{:S(2)}) copy-start(bf16[1024,1024]{1,0:T(8,128)(2,1)} %param.19) | copy-start | bytes 6291460
  0.6 4.8 %copy-start.7 = (s32[1,8]{1,0:T(1,128)S(1)}, s32[1,8]{1,0:T(1,128)}, u32[]{:S(2)}) copy-start(s32[1,8]{1,0:T(1,128)} %param.16) | copy-start | bytes 100
  0.7 5.2 %copy-start.3 = (s32[384]{0:T(512)S(1)}, s32[384]{0:T(512)}, u32[]{:S(2)}) copy-start(s32[384]{0:T(512)} %param.15) | copy-start | bytes 4612
  0.7 5.2 %copy-start.5 = (bf16[16,256]{1,0:T(8,128)(2,1)S(1)}, bf16[16,256]{1,0:T(8,128)(2,1)}, u32[]{:S(2)}) copy-start(bf16[16,256]{1,0:T(8,128)(2,1)} %param.17) | copy-start | bytes 24580
  0.7 6.2 %copy-start.4 = (s32[384]{0:T(512)S(1)}, s32[384]{0:T(512)}, u32[]{:S(2)}) copy-start(s32[384]{0:T(512)} %param.14) | copy-start | bytes 4612
  1.6 5.5 %copy-start.1 = (bf16[256,1024]{1,0:T(8,128)(2,1)S(1)}, bf16[256,1024]{1,0:T(8,128)(2,1)}, u32[]{:S(2)}) copy-start(bf16[256,1024]{1,0:T(8,128)(2,1)} %param.18) | copy-start | bytes 1572868
  3.3 3.6 %collective-permute-start = (bf16[96,256]{1,0:T(8,128)(2,1)S(1)}, bf16[96,256]{1,0:T(8,128)(2,1)S(1)}, u32[]{:S(2)}, u32[]{:S(2)}) collective-permute-start(bf16[96,256]{1,0:T(8,128)(2,1)S(1)} %broadcast_select_fusion.3), channel_id=1, source_target_pairs={{0,2},{2,0},{1,3},{3,1},{4,6},{6,4},{5,7},{7,5},{8,10},{10,8},{9,1... | collective-permute-start | bytes 147464 | tf_op jit(solution)/shard_map/ppermute | solution.py:398
  10.3 1.1 %copy-start.2 = (bf16[384,1024]{1,0:T(8,128)(2,1)S(1)}, bf16[384,1024]{1,0:T(8,128)(2,1)}, u32[]{:S(2)}) copy-start(bf16[384,1024]{1,0:T(8,128)(2,1)} %param.21) | copy-start | bytes 2359300
  10.3 1.3 %copy-start.8 = (bf16[256,1024]{1,0:T(8,128)(2,1)S(1)}, bf16[256,1024]{1,0:T(8,128)(2,1)}, u32[]{:S(2)}) copy-start(bf16[256,1024]{1,0:T(8,128)(2,1)} %param.20) | copy-start | bytes 1572868
  70.6 1.7 %copy-start.6 = (s32[1,192]{1,0:T(1,128)S(1)}, s32[1,192]{1,0:T(1,128)}, u32[]{:S(2)}) copy-start(s32[1,192]{1,0:T(1,128)} %param.12) | copy-start | bytes 2308
